TPU v7x, 512 devices: a whole 4x8x8 slice. The times are simulated.
512 devices in a mesh: grp: 8 (over x, core), leaf: 64 (over y, z).
Axes of the slice: x: 4, y: 8, z: 8, core: 2. Of those that a mesh axis runs over, the one named last changes fastest.
Arguments:
- points: bfloat16 [262144, 64], P(('grp', 'leaf')), may hold values from -0.75 to 0.75
- weights: bfloat16 [262144, 32], P(('grp', 'leaf')), may hold values from -0.0625 to 0.0625
- interp: bfloat16 [262144, 1024], P(('grp', 'leaf')), may hold values from -0.03125 to 0.03125
- near_leaf: int32 [512, 16], P('grp'), may hold values from 0 to 63, as said below
- near_count: int32 [512], P('grp'), may hold values from 1 to 16, as said below
- skel_index: int32 [8, 1024], P('grp'), may hold values from 0 to 32767, as said below
Outputs:
- potential: float32 [262144, 32], P(('grp', 'leaf'))
Inputs may be any that keep to these rules, and one draw needn't show every extreme that they name: `near_leaf`: each row holds distinct leaves; the first entry is the leaf itself. `near_count`: in every group some leaf uses all 16 slots. `skel_index`: each row holds distinct point numbers.
All inputs are finite; a program needn't handle non-finite values.
Results may differ from a plain program's by a relative error of at most 0.0038.
Values may be sent and summed in bfloat16 or wider, within the bound.
A program may use at most 64 MiB of HBM per device.

v0:
```python
import jax
import jax.numpy as jnp
from jax import lax
from jax.sharding import PartitionSpec as P

GAMMA = 0.5


def kernel_apply(targets, sources, source_wts):
    tnorm = jnp.sum(targets.astype(jnp.float32) ** 2, axis=1)
    snorm = jnp.sum(sources.astype(jnp.float32) ** 2, axis=1)
    cross = lax.dot_general(
        targets, sources, (((1,), (1,)), ((), ())), preferred_element_type=jnp.float32
    )
    kern = jnp.exp(-GAMMA * (tnorm[:, None] + snorm[None, :] - 2.0 * cross)).astype(jnp.bfloat16)
    return jnp.dot(kern, source_wts, preferred_element_type=jnp.float32)


def per_device(points, weights, interp, near_leaf, near_count, skel_index):
    rows = points.shape[0]
    columns = weights.shape[1]
    slots = near_leaf.shape[1]
    skel_size = skel_index.shape[1]
    leaf_self = lax.axis_index("leaf")
    group_total = lax.axis_size("grp")
    group_self = lax.axis_index("grp")
    group_pts, group_wts = (
        lax.all_gather(points, "leaf", axis=0, tiled=True),
        lax.all_gather(weights, "leaf", axis=0, tiled=True),
    )

    def block_sum(targets, source):
        start = source * rows
        source_pts = lax.dynamic_slice_in_dim(group_pts, start, rows, 0)
        source_wts = lax.dynamic_slice_in_dim(group_wts, start, rows, 0)
        return kernel_apply(targets, source_pts, source_wts)

    own_list = lax.dynamic_index_in_dim(near_leaf, leaf_self, 0, keepdims=False)
    own_count = lax.dynamic_index_in_dim(near_count, leaf_self, 0, keepdims=False)

    def owner_step(slot, total):
        source = own_list[slot]
        return lax.cond(
            slot < own_count, lambda acc: acc + block_sum(points, source), lambda acc: acc, total
        )

    near = lax.fori_loop(0, slots, owner_step, jnp.zeros((rows, columns), jnp.float32))
    wts_part = lax.dot_general(
        interp, weights, (((0,), (0,)), ((), ())), preferred_element_type=jnp.float32
    )
    skel_local = jnp.take(group_pts, skel_index[0], axis=0)
    wts_grp = lax.psum(wts_part, "leaf")
    skel_bf, wts_bf = (
        lax.all_gather(skel_local, "grp", axis=0, tiled=True),
        lax.all_gather(wts_grp.astype(jnp.bfloat16), "grp", axis=0, tiled=True),
    )

    def far_step(other, total):
        start = other * skel_size
        piece = kernel_apply(
            points,
            lax.dynamic_slice_in_dim(skel_bf, start, skel_size, 0),
            lax.dynamic_slice_in_dim(wts_bf, start, skel_size, 0),
        )
        return total + jnp.where(other != group_self, piece, jnp.zeros_like(piece))

    return lax.fori_loop(0, group_total, far_step, near)


def solution(mesh):
    placed = (
        P(("grp", "leaf"), None),
        P(("grp", "leaf"), None),
        P(("grp", "leaf"), None),
        P("grp", None),
        P("grp"),
        P("grp", None),
    )
    return jax.shard_map(
        per_device, mesh=mesh, in_specs=placed, out_specs=P(("grp", "leaf"), None), check_vma=False
    )
```

profile of v0, /device:TPU:4, one launch (start us, length us, event | category | flops | bytes accessed | tf_op | source)
XLA Modules:
  0.0 522.0 jit_solution(6110924345499895906)
XLA Ops:
  6.5 1.7 copy.13
  8.3 1.5 copy.12
  11.3 103.1 %all-gather.4.cloned.1.call-done = bf16[32768,64]{1,0:T(8,128)(2,1)} async-done(((bf16[512,64]{1,0:T(8,128)(2,1)}), bf16[32768,64]{1,0:T(8,128)(2,1)}) %all-gather.4.cloned.1.call-update) | async-done | bytes 4194320 | tf_op jit(solution)/shard_map/all_gather | solution.py:28
  114.4 7.3 %gather_fusion = bf16[1024,64]{1,0:T(8,128)(2,1)S(1)} fusion(bf16[32768,64]{1,0:T(8,128)(2,1)} %all-gather.4.cloned.1.call-done, s32[1024]{0:T(1024)S(1)} %broadcast_clamp_fusion), kind=kCustom, calls=%fused_computation | custom fusion | bytes 266240 | tf_op jit(solution)/shard_map/jit(_take)/gather | solution.py:51
  123.9 278.5 %all-reduce.1 = bf16[1024,32]{0,1:T(8,128)(2,1)S(1)} all-reduce(f32[1024,32]{0,1:T(8,128)S(1)} %fusion.36), channel_id=1, replica_groups=mesh['grp'=8,'leaf'=64] {'leaf'}, use_global_device_ids=true, to_apply=%region_6.7 | all-reduce | flops 32768 | bytes 196608 | tf_op jit(solution)/shard_map/psum | solution.py:52
  402.3 11.9 %all_gather.15 = bf16[8192,32]{0,1:T(8,128)(2,1)S(1)} all-gather(bf16[1024,32]{0,1:T(8,128)(2,1)S(1)} %all-reduce.1), channel_id=1, replica_groups=mesh['grp'=8,'leaf'=64] {'grp'}, dimensions={0}, use_global_device_ids=true | all-gather | bytes 589824 | tf_op jit(solution)/shard_map/all_gather | solution.py:55
  414.2 76.0 %while.29 = (s32[]{:T(128)}, f32[512,32]{0,1:T(8,128)S(1)}, s32[]{:T(128)}, bf16[512,64]{1,0:T(8,128)(2,1)S(1)}, s32[16]{0:T(128)S(1)}, /*index=5*/bf16[32768,64]{1,0:T(8,128)(2,1)}, bf16[32768,32]{1,0:T(8,128)(2,1)}, s32[]{:T(128)}) while((s32[]{:T(128)}, f32[512,32]{0,1:T(8,128)S(1)}, s32[]{:T(128)}, bf16[512,64]{1,0:T(8,128)(2,1)S(1)}, ...), condition=%wide.region_5.6_spmd, body=%wide.region_0.5_spmd.sunk | while | flops 51854348 | bytes 599291 | solution.py:47
  415.0 4.1 conditional.2
  416.3 1.1 multiply_reduce_fusion
  417.5 1.5 fusion.6
  419.7 4.0 conditional.2
  422.2 1.5 fusion.6
  424.5 4.0 conditional.2
  425.8 1.1 multiply_reduce_fusion
  427.0 1.5 fusion.6
  429.2 4.0 conditional.2
  430.6 1.1 multiply_reduce_fusion
  431.7 1.5 fusion.6
  434.0 4.0 conditional.2
  435.3 1.1 multiply_reduce_fusion
  436.5 1.5 fusion.6
  438.7 4.0 conditional.2
  440.1 1.1 multiply_reduce_fusion
  441.2 1.5 fusion.6
  443.5 4.0 conditional.2
  444.8 1.1 multiply_reduce_fusion
  446.0 1.5 fusion.6
  448.2 4.0 conditional.2
  449.6 1.1 multiply_reduce_fusion
  450.7 1.5 fusion.6
  453.0 4.0 conditional.2
  454.3 1.1 multiply_reduce_fusion
  455.5 1.5 fusion.6
  457.7 4.0 conditional.2
  460.2 1.5 fusion.6
  462.5 4.0 conditional.2
  465.0 1.5 fusion.6
  467.2 4.0 conditional.2
  469.7 1.5 fusion.6
  472.0 4.0 conditional.2
  474.5 1.5 fusion.6
  476.7 4.0 conditional.2
  479.2 1.5 fusion.6
  481.5 4.0 conditional.2
  484.0 1.5 fusion.6
  486.2 4.0 conditional.2
  488.7 1.5 fusion.6
  490.3 24.5 %while.30 = (s32[]{:T(128)}, f32[512,32]{0,1:T(8,128)S(1)}, s32[]{:T(128)}, bf16[512,64]{0,1:T(8,128)(2,1)S(1)}, bf16[8192,64]{1,0:T(8,128)(2,1)}, /*index=5*/bf...) while((s32[]{:T(128)}, f32[512,32]{0,1:T(8,128)S(1)}, s32[]{:T(128)}, ...), condition=%wide.region_10.11_spmd, body=%wide.region_7.10_spmd.sunk | while | flops 103610888 | bytes 734880 | solution.py:67
  490.3 1.2 multiply_reduce_fusion.6
  491.5 1.8 fusion.48
  493.4 1.2 multiply_reduce_fusion.6
  494.6 1.8 fusion.48
  496.5 1.2 multiply_reduce_fusion.6
  497.7 1.8 fusion.48
  499.5 1.2 multiply_reduce_fusion.6
  500.7 1.8 fusion.48
  502.6 1.2 multiply_reduce_fusion.6
  503.8 1.8 fusion.48
  505.7 1.2 multiply_reduce_fusion.6
  506.9 1.8 fusion.48
  508.7 1.2 multiply_reduce_fusion.6
  509.9 1.8 fusion.48
  511.8 1.2 multiply_reduce_fusion.6
  513.0 1.8 fusion.48
  (62 shorter events, 24.2 us)
Async XLA Ops:
  6.5 116.2 %copy-start = (bf16[512,1024]{1,0:T(8,128)(2,1)S(1)}, bf16[512,1024]{1,0:T(8,128)(2,1)}, u32[]{:S(2)}) copy-start(bf16[512,1024]{1,0:T(8,128)(2,1)} %param.14) | copy-start | bytes 3145732
  6.5 116.2 %copy-start.3 = (bf16[512,32]{0,1:T(8,128)(2,1)S(1)}, bf16[512,32]{0,1:T(8,128)(2,1)}, u32[]{:S(2)}) copy-start(bf16[512,32]{0,1:T(8,128)(2,1)} %param.13) | copy-start | bytes 98308
  6.5 107.9 %all-gather.4.cloned.1.call-start = ((), (), s32[]{:S(2)}) async-start(), calls=%async_computation | async-start | bytes 8519680 | tf_op jit(solution)/shard_map/all_gather | solution.py:28
  8.2 406.0 %all-gather.6.cloned.1.call-start = ((), (), s32[]{:S(2)}) async-start(), calls=%async_computation.1 | async-start | bytes 8519680 | tf_op jit(solution)/shard_map/all_gather | solution.py:29
  9.8 480.5 %all-gather.8.cloned.1.call-start = ((), (), s32[]{:S(2)}) async-start(), calls=%async_computation.2 | async-start | bytes 2359296 | tf_op jit(solution)/shard_map/all_gather | solution.py:54
  11.3 111.7 %copy-start.6 = (s32[64]{0:T(128)S(1)}, s32[64]{0:T(128)}, u32[]{:S(2)}) copy-start(s32[64]{0:T(128)} %param.16) | copy-start | bytes 772
  11.3 112.4 %copy-start.5 = (s32[64,16]{0,1:T(8,128)S(1)}, s32[64,16]{0,1:T(8,128)}, u32[]{:S(2)}) copy-start(s32[64,16]{0,1:T(8,128)} %param.15) | copy-start | bytes 12292
  11.3 402.9 %copy-start.1 = (bf16[512,64]{1,0:T(8,128)(2,1)S(1)}, bf16[512,64]{1,0:T(8,128)(2,1)}, u32[]{:S(2)}) copy-start(bf16[512,64]{1,0:T(8,128)(2,1)} %copy.13) | copy-start | bytes 196612
  414.2 76.1 %copy-start.2 = (bf16[512,64]{0,1:T(8,128)(2,1)S(1)}, bf16[512,64]{0,1:T(8,128)(2,1)}, u32[]{:S(2)}) copy-start(bf16[512,64]{0,1:T(8,128)(2,1)} %param.12) | copy-start | bytes 196612
  514.8 0.6 copy-start.4
Sparse Core Ops, SparseCore 0:
  10.4 103.9 all-gather.3
  117.4 98.3 all-gather.5
  218.0 27.5 all-gather.7
where the time goes:
time: 524 us; the launch traced here: 522 us
  blocking collectives  290 us (55%)
  waiting for transfers between devices  103 us (20%)
  matrix products  39.4 us (8%)
  other arithmetic  29.9 us (6%)
  loops' own time  23.2 us (4%)
  local copies, waits for them, and re-layouts  22.7 us (4%)
  between operations  13.2 us (3%)
    psum x1, blocking collectives, per_device(): wts_grp = lax.psum(wts_part, 'leaf')  278 us
    all_gather x1, waiting for transfers between devices, per_device(): lax.all_gather(points, 'leaf', axis=0, tiled=True)  103 us
    dot_general x24, matrix products, kernel_apply(): return jnp.dot(kern, source_wts, preferred_element_type=jnp.float32)  39.1 us
    reduce_sum x24, other arithmetic, kernel_apply(): snorm = jnp.sum(sources.astype(jnp.float32) ** 2, axis=1)  27.3 us
    all_gather x1, blocking collectives, per_device(): lax.all_gather(wts_grp.astype(jnp.bfloat16), 'grp', axis=0, tiled=True)  11.9 us
    another operation x16, loops' own time, owner_step(): lax.cond(slot < own_count, lambda acc: acc + block_sum(points, source), l...  11.6 us
    another operation x1, loops' own time, per_device(): lax.fori_loop(0, slots, owner_step, jnp.zeros((rows, columns), jnp.float32))  11.2 us
    dynamic_slice x16, local copies, waits for them, and re-layouts, owner_step(): source = own_list[slot]  10.6 us
  transfers between devices with their start and end apart: 3, of which 1 were waited for; matrix products, arithmetic and copies ran while one was open for 13% of the time, Pallas kernels for 0%

commit v1 on v0

v1 whole, which is shorter than its diff:
```python
import functools
import heapq

import jax
import jax.numpy as jnp
from jax import lax
from jax.experimental import pallas as pl
from jax.experimental.pallas import tpu as pltpu
from jax.sharding import PartitionSpec as P

MESH = pl.DeviceIdType.MESH
BF, F32 = jnp.bfloat16, jnp.float32
SIDE = 8
PTS, FEAT, COLS, SKEL, SLOTS = 512, 64, 32, 1024, 16
ROWS = FEAT + COLS
HALF = ROWS // 2
PIECE = SKEL // SIDE

FIRST = ((4, 3), (3, 4))


def second(o):
    return (4, 3) if o & 1 else (3, 4)


def hops(half, o1, o2):
    out = []
    if o2 == 0:
        if o1 <= 0 and -o1 < FIRST[half][0]:
            out.append((0, 1))
        if o1 >= 0 and o1 < FIRST[half][1]:
            out.append((0, -1))
        out += [(1, 1), (1, -1)]
    else:
        plus, minus = second(o1)
        if o2 < 0 and -o2 < plus:
            out.append((1, 1))
        if o2 > 0 and o2 < minus:
            out.append((1, -1))
    return out


def schedule():
    free, events, order, count = {}, [], [], 0

    def forward(now, half, o1, o2):
        nonlocal count
        for leg, sign in hops(half, o1, o2):
            link = ((half + leg) % 2, sign)
            begin = max(now, free.get(link, 0.0))
            free[link] = begin + 1.0
            count += 1
            seen = (o1 - sign, o2) if leg == 0 else (o1, o2 - sign)
            heapq.heappush(events, (begin + 2.0, count, half) + seen)

    for half in (0, 1):
        forward(0.0, half, 0, 0)
    while events:
        now, _, half, o1, o2 = heapq.heappop(events)
        order.append((half, o1, o2))
        forward(now, half, o1, o2)
    return order


def slot_of(half, o1, o2):
    oz, oy = (o1, o2) if half == 0 else (o2, o1)
    return (oy % SIDE) * SIDE + oz % SIDE


def split3(v):
    hi = v.astype(BF).astype(F32)
    mid = (v - hi).astype(BF).astype(F32)
    return hi, mid, v - hi - mid


def aug_rows(v, first):
    hi, mid, lo = split3(v)
    row = lax.broadcasted_iota(jnp.int32, (16, v.shape[1]), 0)
    k = row - 3 * first
    terms = jnp.where(k == 0, hi, jnp.where(k == 1, mid, lo))
    mine = (k >= 0) & (k < 3)
    return jnp.where(mine, terms, jnp.where(row < 6, 1.0, 0.0)).astype(BF)


def half_norm(xt):
    xf = xt.astype(F32)
    return -0.5 * jnp.sum(xf * xf, axis=0, keepdims=True)


def kernel(
    near_ref, count_ref, skel_idx, pts_ref, wts_ref, interp_ref, out_ref,
    gat, interp_v, part, got_z, mid, got_y, skel, lhs, acc,
    loc, g_send, g_recv, s_send, s_recv, x_recv,
):
    grp, leaf = lax.axis_index("grp"), lax.axis_index("leaf")
    x, core = grp // 2, grp % 2
    y, z = leaf // SIDE, leaf % SIDE

    def at_leaf(oy, oz):
        return (grp, ((y + oy) % SIDE) * SIDE + (z + oz) % SIDE)

    def at_grp(ox, oc):
        return (((x + ox) % 4) * 2 + (core + oc) % 2, leaf)

    own = [
        pltpu.make_async_copy(pts_ref, gat.at[0, pl.ds(0, FEAT)], loc.at[0]),
        pltpu.make_async_copy(wts_ref, gat.at[0, pl.ds(FEAT, COLS)], loc.at[1]),
        pltpu.make_async_copy(interp_ref, interp_v, loc.at[2]),
    ]
    for c in own:
        c.start()
    barrier = pltpu.get_barrier_semaphore()
    peers = [at_leaf(0, o) for o in range(1, SIDE)] + [at_leaf(o, 0) for o in range(1, SIDE)]
    peers += [at_grp(o, 0) for o in range(1, 4)] + [at_grp(0, 1)]
    for peer in peers:
        pl.semaphore_signal(barrier, inc=1, device_id=peer, device_id_type=MESH)
    own[0].wait()
    own[1].wait()
    pl.semaphore_wait(barrier, len(peers))

    def remote(src, dst, send, recv, peer):
        pltpu.make_async_remote_copy(
            src_ref=src, dst_ref=dst, send_sem=send, recv_sem=recv,
            device_id=peer, device_id_type=MESH,
        ).start()

    def forward(half, o1, o2):
        here = slot_of(half, o1, o2)
        rows = pl.ds(half * HALF, HALF)
        for leg, sign in hops(half, o1, o2):
            there = slot_of(half, *((o1 - sign, o2) if leg == 0 else (o1, o2 - sign)))
            peer = at_leaf(0, sign) if (half + leg) % 2 == 0 else at_leaf(sign, 0)
            remote(gat.at[here, rows], gat.at[there, rows], g_send, g_recv.at[half, there], peer)

    def arrive(half, o1, o2):
        here = slot_of(half, o1, o2)
        ref = gat.at[here, pl.ds(half * HALF, HALF)]
        pltpu.make_async_copy(ref, ref, g_recv.at[half, here]).wait()
        forward(half, o1, o2)

    def whole(ref, sem):
        pltpu.make_async_copy(ref, ref, sem).wait()

    for half in (0, 1):
        forward(half, 0, 0)

    def skel_part():
        own[2].wait()
        index = skel_idx[...] - leaf * PTS
        pick = lax.broadcasted_iota(jnp.int32, (PTS, SKEL), 0) == index
        pts = jnp.dot(gat[0, :FEAT], pick.astype(BF), preferred_element_type=F32).astype(BF)
        wts = jnp.dot(gat[0, FEAT:], interp_v[...], preferred_element_type=F32)
        hi = wts.astype(BF)
        lo = (wts - hi.astype(F32)).astype(BF)
        for k in range(SIDE):
            cols = slice(k * PIECE, (k + 1) * PIECE)
            part[k, :FEAT] = pts[:, cols]
            part[k, FEAT:ROWS] = hi[:, cols]
            part[k, ROWS:] = lo[:, cols]
        for o in range(1, SIDE):
            remote(part.at[(z + o) % SIDE], got_z.at[7 - o], s_send.at[0], s_recv.at[0], at_leaf(0, o))

    def total(first, got):
        def add(k, carry):
            p, w = carry
            v = got[k].astype(F32)
            return p + v[:FEAT], w + v[FEAT:ROWS] + v[ROWS:]

        v = first.astype(F32)
        return lax.fori_loop(0, SIDE - 1, add, (v[:FEAT], v[FEAT:ROWS] + v[ROWS:]))

    def skel_z():
        whole(got_z, s_recv.at[0])
        p, w = total(part[z], got_z)
        hi = w.astype(BF)
        mid[:FEAT] = p.astype(BF)
        mid[FEAT:ROWS] = hi
        mid[ROWS:] = (w - hi.astype(F32)).astype(BF)
        for o in range(1, SIDE):
            remote(mid, got_y.at[7 - o], s_send.at[1], s_recv.at[1], at_leaf(o, 0))

    def skel_y():
        whole(got_y, s_recv.at[1])
        p, w = total(mid[...], got_y)
        skel[0, z, :FEAT] = p.astype(BF)
        skel[0, z, FEAT:] = w.astype(BF)
        for o in range(1, SIDE):
            remote(skel.at[0, z], skel.at[0, z], s_send.at[2], s_recv.at[2], at_leaf(0, o))

    def skel_own():
        whole(skel.at[0, pl.ds(0, 7)], s_recv.at[2])
        for o in (1, 3, 2):
            there = ((4 - o) % 4) * 2
            remote(skel.at[0], skel.at[there], s_send.at[3], x_recv.at[there], at_grp(o, 0))
        remote(skel.at[0], skel.at[1], s_send.at[3], x_recv.at[1], at_grp(0, 1))

    def skel_x(o):
        whole(skel.at[2 * o], x_recv.at[2 * o])
        remote(skel.at[2 * o], skel.at[2 * o + 1], s_send.at[3], x_recv.at[2 * o + 1], at_grp(0, 1))

    def block(xs, ws):
        rhs = jnp.concatenate([xs, aug_rows(half_norm(xs), 0)], axis=0)
        arg = jnp.dot(lhs[...], rhs, preferred_element_type=F32)
        kern = jnp.exp(arg).astype(BF)
        acc[...] += lax.dot_general(kern, ws, (((1,), (1,)), ((), ())), preferred_element_type=F32)

    def targets():
        xt = gat[0, :FEAT]
        rows = jnp.concatenate([xt, aug_rows(half_norm(xt), 1)], axis=0)
        pad = jnp.zeros((128 - rows.shape[0], PTS), F32)
        turned = jnp.concatenate([rows.astype(F32), pad], axis=0).T
        lhs[...] = turned[:, :FEAT + 16].astype(BF)
        acc[...] = jnp.zeros_like(acc)

    def far(rel):
        whole_it = rel % 2 == 1
        if whole_it:
            whole(skel.at[rel], x_recv.at[rel])

        @pl.loop(0, 2)
        def _(k):
            both = jnp.concatenate([skel[rel, 4 * k + i] for i in range(4)], axis=1)
            block(both[:FEAT], both[FEAT:])

    order = schedule()
    steps = {
        0: [skel_part], 8: [targets], 14: [skel_z], 26: [skel_y], 40: [skel_own],
        66: [lambda: far(1)], 74: [lambda: skel_x(1)], 76: [lambda: skel_x(3)],
        82: [lambda: far(2)], 88: [lambda: far(6)], 92: [lambda: skel_x(2)],
        94: [lambda: far(3)], 100: [lambda: far(7)], 106: [lambda: far(4)], 112: [lambda: far(5)],
    }
    for i, event in enumerate(order):
        for f in steps.get(i, ()):
            f()
        arrive(*event)

    mine = count_ref[leaf]

    @pl.loop(0, SLOTS)
    def _(k):
        source = near_ref[k, leaf]
        sy = (source // SIDE + SIDE - y) % SIDE
        sz = (source % SIDE + SIDE - z) % SIDE
        got = gat[sy * SIDE + sz]
        used = jnp.where(k < mine, 1.0, 0.0).astype(F32)
        block(got[:FEAT], (got[FEAT:].astype(F32) * used).astype(BF))

    pad = jnp.zeros((PTS, 128 - COLS), F32)
    out_ref[...] = jnp.concatenate([acc[...], pad], axis=1).T[:COLS]

    sent = gat.at[pl.ds(0, 63)]
    pltpu.make_async_copy(sent, sent, g_send).wait()
    for i, ref in enumerate((got_z, got_y, skel.at[0, pl.ds(0, 7)], skel.at[pl.ds(0, 7)])):
        whole(ref, s_send.at[i])


def per_device(points, weights, interp, near_leaf, near_count, skel_index):
    flops = 2 * 30 * PTS * PTS * (FEAT + 16 + COLS) + 2 * PTS * SKEL * ROWS
    out = pl.pallas_call(
        kernel,
        out_shape=jax.ShapeDtypeStruct((COLS, PTS), F32),
        in_specs=[
            pl.BlockSpec(memory_space=pltpu.SMEM),
            pl.BlockSpec(memory_space=pltpu.SMEM),
            pl.BlockSpec(memory_space=pltpu.VMEM),
            pl.BlockSpec(memory_space=pl.ANY),
            pl.BlockSpec(memory_space=pl.ANY),
            pl.BlockSpec(memory_space=pl.ANY),
        ],
        out_specs=pl.BlockSpec(memory_space=pltpu.VMEM),
        scratch_shapes=[
            pltpu.VMEM((64, ROWS, PTS), BF),
            pltpu.VMEM((PTS, SKEL), BF),
            pltpu.VMEM((SIDE, ROWS + COLS, PIECE), BF),
            pltpu.VMEM((SIDE - 1, ROWS + COLS, PIECE), BF),
            pltpu.VMEM((ROWS + COLS, PIECE), BF),
            pltpu.VMEM((SIDE - 1, ROWS + COLS, PIECE), BF),
            pltpu.VMEM((8, SIDE, ROWS, PIECE), BF),
            pltpu.VMEM((PTS, FEAT + 16), BF),
            pltpu.VMEM((PTS, COLS), F32),
            pltpu.SemaphoreType.DMA((3,)),
            pltpu.SemaphoreType.DMA,
            pltpu.SemaphoreType.DMA((2, 64)),
            pltpu.SemaphoreType.DMA((4,)),
            pltpu.SemaphoreType.DMA((3,)),
            pltpu.SemaphoreType.DMA((8,)),
        ],
        cost_estimate=pl.CostEstimate(
            flops=flops, bytes_accessed=2 * PTS * SKEL, transcendentals=30 * PTS * PTS
        ),
        compiler_params=pltpu.CompilerParams(
            collective_id=0, has_side_effects=True, vmem_limit_bytes=48 * 1024 * 1024
        ),
    )(near_leaf.T, near_count, skel_index, points.T, weights.T, interp)
    return out.T


def solution(mesh):
    placed = (
        P(("grp", "leaf"), None),
        P(("grp", "leaf"), None),
        P(("grp", "leaf"), None),
        P("grp", None),
        P("grp"),
        P("grp", None),
    )
    return jax.shard_map(
        per_device, mesh=mesh, in_specs=placed, out_specs=P(("grp", "leaf"), None), check_vma=False
    )
```

time: 524 us -> 82.5 us (0.16)
  the two profiles are of different devices: /device:TPU:4 before, /device:TPU:6 now
where the time goes in v1:
time: 82.5 us; the launch traced here: 82.1 us
  Pallas kernels  77.3 us (94%)
  local copies, waits for them, and re-layouts  4.84 us (6%)
    pallas_call x1, Pallas kernels, per_device(): pl.pallas_call(kernel, out_shape=jax.ShapeDtypeStruct((COLS, PTS), F32),...  77.3 us
    unnamed x13, local copies, waits for them, and re-layouts  4.84 us

profile of v1, /device:TPU:6, one launch (start us, length us, event | category | flops | bytes accessed | tf_op | source)
XLA Modules:
  0.0 82.1 jit_solution(14287562045171086043)
XLA Ops:
  0.0 0.0 copy-start.4
  0.0 0.0 copy-start.5
  0.0 0.7 copy-done.4
  0.7 0.0 copy-done.5
  0.7 0.0 copy-start
  0.7 1.2 %copy-done = bf16[512,1024]{1,0:T(8,128)(2,1)S(1)} copy-done((bf16[512,1024]{1,0:T(8,128)(2,1)S(1)}, bf16[512,1024]{1,0:T(8,128)(2,1)}, u32[]{:S(2)}) %copy-start) | copy-done | bytes 1048600
  1.9 0.0 copy-start.1
  1.9 0.8 %copy-done.1 = bf16[512,64]{0,1:T(8,128)(2,1)S(1)} copy-done((bf16[512,64]{0,1:T(8,128)(2,1)S(1)}, bf16[512,64]{0,1:T(8,128)(2,1)}, u32[]{:S(2)}) %copy-start.1) | copy-done | bytes 65560
  2.8 0.0 copy-start.2
  2.8 0.8 copy-done.2
  3.5 0.0 copy-start.3
  3.5 0.7 copy-done.3
  4.2 77.3 %shard_map.64 = f32[32,512]{1,0:T(8,128)S(1)} custom-call(s32[16,64]{1,0:T(8,128)S(1)} %bitcast.7, s32[64]{0:T(128)S(1)} %copy-done.5, s32[1,1024]{1,0:T(1,128)S(1)} %copy-done.4, bf16[64,512]{1,0:T(8,128)(2,1)S(1)} %bitcast.5, bf16[32,512]{1,0:T(8,128)(2,1)S(1)} %bitcast.6, bf16[512,1024]{1,0:T(8,128)(2,1)S(1)} %copy-done), custom_call_target="tpu_custom_call" | custom-call | flops 1862270976 | bytes 1048576 | tf_op jit(solution)/shard_map/pallas_call | solution.py:259
  81.5 0.6 copy.8
Async XLA Ops:
  0.0 0.7 copy-start.4
  0.0 0.7 copy-start.5
  0.7 1.2 %copy-start = (bf16[512,1024]{1,0:T(8,128)(2,1)S(1)}, bf16[512,1024]{1,0:T(8,128)(2,1)}, u32[]{:S(2)}) copy-start(bf16[512,1024]{1,0:T(8,128)(2,1)} %interp_ref.1) | copy-start | bytes 3145732
  1.9 0.8 %copy-start.1 = (bf16[512,64]{0,1:T(8,128)(2,1)S(1)}, bf16[512,64]{0,1:T(8,128)(2,1)}, u32[]{:S(2)}) copy-start(bf16[512,64]{0,1:T(8,128)(2,1)} %param.6) | copy-start | bytes 196612
  2.8 0.8 copy-start.2
  3.5 0.7 copy-start.3

commit v2 on v1

v2 whole, which is shorter than its diff:
```python
import functools
import heapq

import jax
import jax.numpy as jnp
from jax import lax
from jax.experimental import pallas as pl
from jax.experimental.pallas import tpu as pltpu
from jax.sharding import PartitionSpec as P

MESH = pl.DeviceIdType.MESH
BF, F32 = jnp.bfloat16, jnp.float32
SIDE = 8
PTS, FEAT, COLS, SKEL, SLOTS = 512, 64, 32, 1024, 16
ROWS = FEAT + COLS
HALF = ROWS // 2
PIECE = SKEL // SIDE

FIRST = ((4, 3), (3, 4))


def second(o):
    return (4, 3) if o & 1 else (3, 4)


def hops(half, o1, o2):
    out = []
    if o2 == 0:
        if o1 <= 0 and -o1 < FIRST[half][0]:
            out.append((0, 1))
        if o1 >= 0 and o1 < FIRST[half][1]:
            out.append((0, -1))
        out += [(1, 1), (1, -1)]
    else:
        plus, minus = second(o1)
        if o2 < 0 and -o2 < plus:
            out.append((1, 1))
        if o2 > 0 and o2 < minus:
            out.append((1, -1))
    return out


CHUNK, HOP, LEAD, STAGE, PART = 0.98, 1.7, 2.0, 3.2, 2.2


def schedule():
    links = [(axis, sign) for axis in (0, 1) for sign in (1, -1)]
    free = {link: 0.0 for link in links}
    queue = {link: [] for link in links}
    arrivals, ready, program = [], [(0.0, 0, "part")], []
    count, now = 0, 0.0

    def left(half, o1, o2, leg, sign):
        reach = FIRST[half] if leg == 0 else second(o1)
        gone = abs(o1) if leg == 0 else abs(o2)
        return reach[0 if sign > 0 else 1] - gone + (4 if leg == 0 else 0)

    def enqueue(half, o1, o2):
        nonlocal count
        for leg, sign in hops(half, o1, o2):
            count += 1
            item = (-left(half, o1, o2, leg, sign), count, half, o1, o2, leg, sign)
            heapq.heappush(queue[((half + leg) % 2, sign)], item)

    def burst(share, after):
        nonlocal count
        end = now
        for axis, sign in links:
            free[axis, sign] = max(now, free[axis, sign]) + 8 * share[axis] * CHUNK
            end = max(end, free[axis, sign])
        count += 1
        heapq.heappush(ready, (end + STAGE, count, after))

    def at(delay, *names):
        nonlocal count
        for name in names:
            count += 1
            heapq.heappush(ready, (now + delay, count, name))

    for half in (0, 1):
        enqueue(half, 0, 0)
    while True:
        if arrivals and arrivals[0][0] <= now:
            _, _, half, o1, o2 = heapq.heappop(arrivals)
            program.append(("wait", half, o1, o2))
            now += 0.04
            enqueue(half, o1, o2)
            continue
        open_links = [k for k in links if queue[k] and free[k] - now <= LEAD]
        if open_links:
            link = min(open_links, key=lambda k: free[k])
            _, _, half, o1, o2, leg, sign = heapq.heappop(queue[link])
            program.append(("send", half, o1, o2, leg, sign))
            free[link] = max(now, free[link]) + CHUNK
            seen = (o1 - sign, o2) if leg == 0 else (o1, o2 - sign)
            count += 1
            heapq.heappush(arrivals, (free[link] + HOP, count, half) + seen)
            now += 0.03
            continue
        if ready and ready[0][0] <= now:
            name = heapq.heappop(ready)[2]
            program.append((name,))
            if name == "part":
                now += PART
                burst((1 / 3, 1 / 3), "sum1")
                at(0.0, "targets")
            elif name == "targets":
                now += 0.6
                at(0.0, "self")
            elif name == "sum1":
                now += 0.3
                burst((1 / 3, 1 / 3), "sum2")
            elif name == "sum2":
                now += 0.3
                burst((1 / 6, 1 / 3), "own")
            elif name == "own":
                at(2.5, "far1")
                at(6.0, "x1", "x3")
            elif name in ("x1", "x3"):
                at(0.5, "far" + {"x1": "2", "x3": "6"}[name])
                at(3.0, "far" + {"x1": "3", "x3": "7"}[name])
                if name == "x3":
                    at(4.2, "x2")
            elif name == "x2":
                at(0.2, "far4")
                at(3.0, "far5")
            else:
                now += 0.36 if name == "self" else 0.72
            continue
        times = [free[k] - LEAD for k in links if queue[k]]
        times += [arrivals[0][0]] if arrivals else []
        times += [ready[0][0]] if ready else []
        if not times:
            return program, now
        now = max(now + 1e-3, min(times))


def slot_of(half, o1, o2):
    oz, oy = (o1, o2) if half == 0 else (o2, o1)
    return (oy % SIDE) * SIDE + oz % SIDE


def split3(v):
    hi = v.astype(BF).astype(F32)
    mid = (v - hi).astype(BF).astype(F32)
    return hi, mid, v - hi - mid


def aug_rows(v, first):
    hi, mid, lo = split3(v)
    row = lax.broadcasted_iota(jnp.int32, (16, v.shape[1]), 0)
    k = row - 3 * first
    terms = jnp.where(k == 0, hi, jnp.where(k == 1, mid, lo))
    mine = (k >= 0) & (k < 3)
    return jnp.where(mine, terms, jnp.where(row < 6, 1.0, 0.0)).astype(BF)


def half_norm(xt):
    xf = xt.astype(F32)
    return -0.5 * jnp.sum(xf * xf, axis=0, keepdims=True)


def kernel(
    near_hbm, count_hbm, index_hbm, pts_ref, wts_ref, interp_ref, out_ref,
    gat, interp_v, near_ref, count_ref, index_v, part, got1, mid, got2, skel, lhs, acc,
    loc, g_send, g_recv, s_send, s_recv, x_recv,
):
    grp, leaf = lax.axis_index("grp"), lax.axis_index("leaf")
    x, core = grp // 2, grp % 2
    y, z = leaf // SIDE, leaf % SIDE

    def at_leaf(oy, oz):
        return (grp, ((y + oy + SIDE) % SIDE) * SIDE + (z + oz + SIDE) % SIDE)

    def at_grp(ox, oc):
        return (((x + ox) % 4) * 2 + (core + oc) % 2, leaf)

    barrier = pltpu.get_barrier_semaphore()
    peers = [at_leaf(0, o) for o in range(1, SIDE)] + [at_leaf(o, 0) for o in range(1, SIDE)]
    peers += [at_grp(1, 0), at_grp(3, 0), at_grp(0, 1)]
    for peer in peers:
        pl.semaphore_signal(barrier, inc=1, device_id=peer, device_id_type=MESH)
    own = [
        pltpu.make_async_copy(pts_ref, gat.at[0, pl.ds(0, FEAT)], loc.at[0]),
        pltpu.make_async_copy(wts_ref, gat.at[0, pl.ds(FEAT, COLS)], loc.at[1]),
        pltpu.make_async_copy(interp_ref, interp_v, loc.at[2]),
        pltpu.make_async_copy(index_hbm, index_v, loc.at[3]),
        pltpu.make_async_copy(near_hbm, near_ref, loc.at[4]),
        pltpu.make_async_copy(count_hbm, count_ref, loc.at[5]),
    ]
    for c in own:
        c.start()
    own[0].wait()
    own[1].wait()
    pl.semaphore_wait(barrier, len(peers))

    def remote(src, dst, send, recv, peer):
        pltpu.make_async_remote_copy(
            src_ref=src, dst_ref=dst, send_sem=send, recv_sem=recv,
            device_id=peer, device_id_type=MESH,
        ).start()

    def whole(ref, sem):
        pltpu.make_async_copy(ref, ref, sem).wait()

    def do_send(half, o1, o2, leg, sign):
        here = slot_of(half, o1, o2)
        there = slot_of(half, *((o1 - sign, o2) if leg == 0 else (o1, o2 - sign)))
        rows = pl.ds(half * HALF, HALF)
        peer = at_leaf(0, sign) if (half + leg) % 2 == 0 else at_leaf(sign, 0)
        remote(gat.at[here, rows], gat.at[there, rows], g_send, g_recv.at[half, there], peer)

    def do_wait(half, o1, o2):
        here = slot_of(half, o1, o2)
        whole(gat.at[here, pl.ds(half * HALF, HALF)], g_recv.at[half, here])

    def exchange(src_of, dst, stage):
        for o in range(1, SIDE):
            for kind in (0, 1):
                along_y = (kind + stage) % 2 == 0
                peer = at_leaf(o, 0) if along_y else at_leaf(0, o)
                remote(src_of(kind, o), dst.at[kind, 7 - o], s_send.at[stage, kind],
                       s_recv.at[stage, kind], peer)

    def do_part():
        own[2].wait()
        own[3].wait()
        index = index_v[...] - leaf * PTS
        pick = lax.broadcasted_iota(jnp.int32, (PTS, SKEL), 0) == index
        pts = jnp.dot(gat[0, :FEAT], pick.astype(BF), preferred_element_type=F32).astype(BF)
        wts = jnp.dot(gat[0, FEAT:], interp_v[...], preferred_element_type=F32)
        hi = wts.astype(BF)
        lo = (wts - hi.astype(F32)).astype(BF)
        for k in range(SIDE):
            cols = slice(k * PIECE, (k + 1) * PIECE)
            part[0, k] = pts[:, cols]
            part[1, k, :COLS] = hi[:, cols]
            part[1, k, COLS:] = lo[:, cols]
        place = (y, z)
        exchange(lambda kind, o: part.at[kind, (place[kind] + o) % SIDE], got1, 0)

    def total(kind, first, got):
        v = first.astype(F32)
        for k in range(SIDE - 1):
            v = v + got[kind, k].astype(F32)
        return v if kind == 0 else v[:COLS] + v[COLS:]

    def do_sum1():
        for kind in (0, 1):
            whole(got1.at[kind], s_recv.at[0, kind])
        mid[0] = total(0, part[0, y], got1).astype(BF)
        w = total(1, part[1, z], got1)
        hi = w.astype(BF)
        mid[1, :COLS] = hi
        mid[1, COLS:] = (w - hi.astype(F32)).astype(BF)
        exchange(lambda kind, o: mid.at[kind], got2, 1)

    def do_sum2():
        for kind in (0, 1):
            whole(got2.at[kind], s_recv.at[1, kind])
        skel[0, y, :FEAT] = total(0, mid[0], got2).astype(BF)
        skel[0, z, FEAT:] = total(1, mid[1], got2).astype(BF)
        p, w = skel.at[0, y, pl.ds(0, FEAT)], skel.at[0, z, pl.ds(FEAT, COLS)]
        for o in range(1, SIDE):
            remote(p, p, s_send.at[2, 0], s_recv.at[2, 0], at_leaf(o, 0))
            remote(w, w, s_send.at[2, 1], s_recv.at[2, 1], at_leaf(0, o))

    others = (skel.at[0, pl.ds(0, 7), pl.ds(0, FEAT)], skel.at[0, pl.ds(0, 7), pl.ds(FEAT, COLS)])

    def do_own():
        for kind in (0, 1):
            whole(others[kind], s_recv.at[2, kind])
        for dx in (1, 3):
            there = 2 * (4 - dx)
            remote(skel.at[0], skel.at[there], s_send.at[3, 0], x_recv.at[there], at_grp(dx, 0))
        remote(skel.at[0], skel.at[1], s_send.at[3, 0], x_recv.at[1], at_grp(0, 1))

    def do_x(dx):
        if dx != 2:
            whole(skel.at[2 * dx], x_recv.at[2 * dx])
            part_of = pl.ds(0 if dx == 1 else 4, 4)
            remote(skel.at[2 * dx, part_of], skel.at[4, part_of], s_send.at[3, 1],
                   x_recv.at[4 if dx == 1 else 8], at_grp(4 - dx, 0))
        else:
            whole(skel.at[4, pl.ds(0, 4)], x_recv.at[4])
            whole(skel.at[4, pl.ds(4, 4)], x_recv.at[8])
        remote(skel.at[2 * dx], skel.at[2 * dx + 1], s_send.at[3, 0], x_recv.at[2 * dx + 1], at_grp(0, 1))

    def block(xs, ws):
        rhs = jnp.concatenate([xs, aug_rows(half_norm(xs), 0)], axis=0)
        arg = jnp.dot(lhs[...], rhs, preferred_element_type=F32)
        kern = jnp.exp(arg).astype(BF)
        return lax.dot_general(kern, ws, (((1,), (1,)), ((), ())), preferred_element_type=F32)

    def do_targets():
        xt = gat[0, :FEAT]
        rows = jnp.concatenate([xt, aug_rows(half_norm(xt), 1)], axis=0)
        pad = jnp.zeros((128 - rows.shape[0], PTS), F32)
        turned = jnp.concatenate([rows.astype(F32), pad], axis=0).T
        lhs[...] = turned[:, :FEAT + 16].astype(BF)

    def do_self():
        acc[...] = block(gat[0, :FEAT], gat[0, FEAT:])

    def do_far(rel):
        if rel % 2 == 1:
            whole(skel.at[rel], x_recv.at[rel])
        both = jnp.concatenate([skel[rel, i] for i in range(SIDE)], axis=1)
        acc[...] += (block(both[:FEAT, :PTS], both[FEAT:, :PTS])
                     + block(both[:FEAT, PTS:], both[FEAT:, PTS:]))

    work = {"wait": do_wait, "send": do_send, "part": do_part, "sum1": do_sum1,
            "sum2": do_sum2, "own": do_own, "targets": do_targets, "self": do_self}
    for dx in (1, 2, 3):
        work["x%d" % dx] = functools.partial(do_x, dx)
    for rel in range(1, 8):
        work["far%d" % rel] = functools.partial(do_far, rel)
    for name, *args in schedule()[0]:
        work[name](*args)

    own[4].wait()
    own[5].wait()
    mine = count_ref[leaf]

    @pl.loop(0, SLOTS // 5)
    def _(i):
        add = jnp.zeros((PTS, COLS), F32)
        for j in range(5):
            k = 1 + 5 * i + j
            source = near_ref[k, leaf]
            sy = (source // SIDE + SIDE - y) % SIDE
            sz = (source % SIDE + SIDE - z) % SIDE
            got = gat[sy * SIDE + sz]
            used = jnp.where(k < mine, 1.0, 0.0).astype(F32)
            add = add + block(got[:FEAT], (got[FEAT:].astype(F32) * used).astype(BF))
        acc[...] += add

    pad = jnp.zeros((PTS, 128 - COLS), F32)
    out_ref[...] = jnp.concatenate([acc[...], pad], axis=1).T[:COLS]

    whole(gat.at[pl.ds(0, 63)], g_send)
    for kind in (0, 1):
        whole(got1.at[kind], s_send.at[0, kind])
        whole(got2.at[kind], s_send.at[1, kind])
        whole(others[kind], s_send.at[2, kind])
    whole(skel.at[pl.ds(0, 6)], s_send.at[3, 0])
    whole(skel.at[0], s_send.at[3, 1])


def per_device(points, weights, interp, near_leaf, near_count, skel_index):
    flops = 2 * 30 * PTS * PTS * (FEAT + 16 + COLS) + 2 * PTS * SKEL * ROWS
    out = pl.pallas_call(
        kernel,
        out_shape=jax.ShapeDtypeStruct((COLS, PTS), F32),
        in_specs=[pl.BlockSpec(memory_space=pltpu.HBM)] * 6,
        out_specs=pl.BlockSpec(memory_space=pltpu.VMEM),
        scratch_shapes=[
            pltpu.VMEM((64, ROWS, PTS), BF),
            pltpu.VMEM((PTS, SKEL), BF),
            pltpu.SMEM((SLOTS, 64), jnp.int32),
            pltpu.SMEM((64,), jnp.int32),
            pltpu.VMEM((1, SKEL), jnp.int32),
            pltpu.VMEM((2, SIDE, FEAT, PIECE), BF),
            pltpu.VMEM((2, SIDE - 1, FEAT, PIECE), BF),
            pltpu.VMEM((2, FEAT, PIECE), BF),
            pltpu.VMEM((2, SIDE - 1, FEAT, PIECE), BF),
            pltpu.VMEM((8, SIDE, ROWS, PIECE), BF),
            pltpu.VMEM((PTS, FEAT + 16), BF),
            pltpu.VMEM((PTS, COLS), F32),
            pltpu.SemaphoreType.DMA((6,)),
            pltpu.SemaphoreType.DMA,
            pltpu.SemaphoreType.DMA((2, 64)),
            pltpu.SemaphoreType.DMA((4, 2)),
            pltpu.SemaphoreType.DMA((3, 2)),
            pltpu.SemaphoreType.DMA((9,)),
        ],
        cost_estimate=pl.CostEstimate(
            flops=flops, bytes_accessed=2 * PTS * SKEL, transcendentals=30 * PTS * PTS
        ),
        compiler_params=pltpu.CompilerParams(
            collective_id=0, has_side_effects=True, vmem_limit_bytes=60 * 1024 * 1024
        ),
    )(near_leaf.T, near_count, skel_index, points.T, weights.T, interp)
    return out.T


def solution(mesh):
    placed = (
        P(("grp", "leaf"), None),
        P(("grp", "leaf"), None),
        P(("grp", "leaf"), None),
        P("grp", None),
        P("grp"),
        P("grp", None),
    )
    return jax.shard_map(
        per_device, mesh=mesh, in_specs=placed, out_specs=P(("grp", "leaf"), None), check_vma=False
    )
```

time: 82.5 us -> 66.2 us (0.80)
  Pallas kernels: 77.3 us -> 64.5 us
  local copies, waits for them, and re-layouts: 4.84 us -> 1.47 us
    pallas_call x1, Pallas kernels: 77.3 us -> 64.5 us  [per_device(): pl.pallas_call(kernel, out_shape=jax.ShapeDtypeStruct((COLS, PTS), F32),...]
    unnamed x13 -> x1, local copies, waits for them, and re-layouts: 4.84 us -> 1.47 us
where the time goes in v2:
time: 66.2 us; the launch traced here: 66 us
  Pallas kernels  64.5 us (97%)
  local copies, waits for them, and re-layouts  1.47 us (2%)
    pallas_call x1, Pallas kernels, per_device(): pl.pallas_call(kernel, out_shape=jax.ShapeDtypeStruct((COLS, PTS), F32),...  64.5 us
    unnamed x1, local copies, waits for them, and re-layouts  1.47 us

profile of v2, /device:TPU:6, one launch (start us, length us, event | category | flops | bytes accessed | tf_op | source)
XLA Modules:
  0.0 66.0 jit_solution(1376981048003163857)
XLA Ops:
  0.0 64.5 %shard_map.64 = f32[32,512]{1,0:T(8,128)} custom-call(s32[16,64]{1,0:T(8,128)} %bitcast.7, s32[64]{0:T(128)} %count_hbm.1, s32[1,1024]{1,0:T(1,128)} %index_hbm.1, bf16[64,512]{1,0:T(8,128)(2,1)} %bitcast.5, bf16[32,512]{1,0:T(8,128)(2,1)} %bitcast.6, bf16[512,1024]{1,0:T(8,128)(2,1)} %interp_ref.1), custom_call_target="tpu_custom_call" | custom-call | flops 1862270976 | bytes 1048576 | tf_op jit(solution)/shard_map/pallas_call | solution.py:352
  64.5 1.5 %copy.8 = f32[512,32]{0,1:T(8,128)} copy(f32[512,32]{0,1:T(8,128)} %bitcast.4) | data formatting | bytes 131072

commit v3 on v2

--- a/solution.py
+++ b/solution.py
@@ -40,7 +40,7 @@
     return out
 
 
-CHUNK, HOP, LEAD, STAGE, PART = 0.98, 1.7, 2.0, 3.2, 2.2
+CHUNK, HOP, LEAD, STAGE, PART = 0.98, 1.7, 2.0, 2.2, 2.2
 
 
 def schedule():
@@ -109,21 +109,25 @@
                 at(0.0, "self")
             elif name == "sum1":
                 now += 0.3
-                burst((1 / 3, 1 / 3), "sum2")
+                burst((1 / 24, 1 / 24), "sum2")
             elif name == "sum2":
-                now += 0.3
+                now += 0.2
+                burst((1 / 24, 1 / 48), "sum3")
+            elif name == "sum3":
                 burst((1 / 6, 1 / 3), "own")
             elif name == "own":
-                at(2.5, "far1")
-                at(6.0, "x1", "x3")
-            elif name in ("x1", "x3"):
-                at(0.5, "far" + {"x1": "2", "x3": "6"}[name])
-                at(3.0, "far" + {"x1": "3", "x3": "7"}[name])
-                if name == "x3":
-                    at(4.2, "x2")
-            elif name == "x2":
+                at(3.0, "far1")
+                at(4.2, "relay1", "relay3")
+                at(6.2, "rest1", "rest3")
+                at(8.6, "last")
+            elif name in ("rest1", "rest3"):
+                at(0.2, "far" + {"rest1": "2", "rest3": "6"}[name])
+                at(2.5, "far" + {"rest1": "3", "rest3": "7"}[name])
+            elif name == "last":
                 at(0.2, "far4")
-                at(3.0, "far5")
+                at(2.5, "far5")
+            elif name in ("relay1", "relay3"):
+                pass
             else:
                 now += 0.36 if name == "self" else 0.72
             continue
@@ -162,7 +166,7 @@
 
 def kernel(
     near_hbm, count_hbm, index_hbm, pts_ref, wts_ref, interp_ref, out_ref,
-    gat, interp_v, near_ref, count_ref, index_v, part, got1, mid, got2, skel, lhs, acc,
+    gat, interp_v, near_ref, count_ref, index_v, part, got1, mid_p, mid_w, got_p, got_w, skel, lhs, acc,
     loc, g_send, g_recv, s_send, s_recv, x_recv,
 ):
     grp, leaf = lax.axis_index("grp"), lax.axis_index("leaf")
@@ -190,8 +194,6 @@
     ]
     for c in own:
         c.start()
-    own[0].wait()
-    own[1].wait()
     pl.semaphore_wait(barrier, len(peers))
 
     def remote(src, dst, send, recv, peer):
@@ -208,23 +210,22 @@
         there = slot_of(half, *((o1 - sign, o2) if leg == 0 else (o1, o2 - sign)))
         rows = pl.ds(half * HALF, HALF)
         peer = at_leaf(0, sign) if (half + leg) % 2 == 0 else at_leaf(sign, 0)
-        remote(gat.at[here, rows], gat.at[there, rows], g_send, g_recv.at[half, there], peer)
+        parts = [(gat.at[here, rows], rows)]
+        if here == 0 and half == 0:
+            parts = [(pts_ref.at[rows], rows)]
+        elif here == 0:
+            last, below = pl.ds(HALF, FEAT - HALF), pl.ds(FEAT, COLS)
+            parts = [(pts_ref.at[last], last), (wts_ref, below)]
+        for src, place in parts:
+            remote(src, gat.at[there, place], g_send, g_recv.at[half, there], peer)
 
     def do_wait(half, o1, o2):
         here = slot_of(half, o1, o2)
         whole(gat.at[here, pl.ds(half * HALF, HALF)], g_recv.at[half, here])
 
-    def exchange(src_of, dst, stage):
-        for o in range(1, SIDE):
-            for kind in (0, 1):
-                along_y = (kind + stage) % 2 == 0
-                peer = at_leaf(o, 0) if along_y else at_leaf(0, o)
-                remote(src_of(kind, o), dst.at[kind, 7 - o], s_send.at[stage, kind],
-                       s_recv.at[stage, kind], peer)
-
     def do_part():
-        own[2].wait()
-        own[3].wait()
+        for c in own[:4]:
+            c.wait()
         index = index_v[...] - leaf * PTS
         pick = lax.broadcasted_iota(jnp.int32, (PTS, SKEL), 0) == index
         pts = jnp.dot(gat[0, :FEAT], pick.astype(BF), preferred_element_type=F32).astype(BF)
@@ -236,8 +237,15 @@
             part[0, k] = pts[:, cols]
             part[1, k, :COLS] = hi[:, cols]
             part[1, k, COLS:] = lo[:, cols]
-        place = (y, z)
-        exchange(lambda kind, o: part.at[kind, (place[kind] + o) % SIDE], got1, 0)
+        for o in range(1, SIDE):
+            for kind, place in ((0, y), (1, z)):
+                remote(part.at[kind, (place + o) % SIDE], got1.at[kind, 7 - o], s_send.at[0, kind],
+                       s_recv.at[0, kind], peer_on(1 - kind, o))
+
+    takes = ((z, 2, y, FEAT // 16), (y, 4, z, COLS // 16))
+
+    def peer_on(kind, o):
+        return at_leaf(0, o) if kind == 0 else at_leaf(o, 0)
 
     def total(kind, first, got):
         v = first.astype(F32)
@@ -248,43 +256,85 @@
     def do_sum1():
         for kind in (0, 1):
             whole(got1.at[kind], s_recv.at[0, kind])
-        mid[0] = total(0, part[0, y], got1).astype(BF)
-        w = total(1, part[1, z], got1)
-        hi = w.astype(BF)
-        mid[1, :COLS] = hi
-        mid[1, COLS:] = (w - hi.astype(F32)).astype(BF)
-        exchange(lambda kind, o: mid.at[kind], got2, 1)
+        mid_p[...] = total(0, part[0, y], got1).astype(BF)
+        mid_w[...] = total(1, part[1, z], got1)
+        for kind, (mid, got) in enumerate(((mid_p, got_p), (mid_w, got_w))):
+            place, every, _, chunks = takes[kind]
+            for c in range(chunks):
+                off = (every * c - place + SIDE) % SIDE
+
+                @pl.when(off != 0)
+                def _():
+                    remote(mid.at[pl.ds(16 * c, 16)], got.at[SIDE - 1 - off], s_send.at[1, kind],
+                           s_recv.at[1, kind], peer_on(kind, off))
 
     def do_sum2():
+        for kind, (mid, got) in enumerate(((mid_p, got_p), (mid_w, got_w))):
+            place, every, piece, _ = takes[kind]
+
+            @pl.when(place % every == 0)
+            def _():
+                whole(got, s_recv.at[1, kind])
+                row = pl.multiple_of(place // every * 16, 16)
+                v = mid[pl.ds(row, 16)].astype(F32)
+                for k in range(SIDE - 1):
+                    v = v + got[k].astype(F32)
+                mine = pl.ds(pl.multiple_of(kind * FEAT + row, 16), 16)
+                skel[0, piece, mine] = v.astype(BF)
+                for o in range(1, SIDE):
+                    ref = skel.at[0, piece, mine]
+                    remote(ref, ref, s_send.at[2, kind], s_recv.at[2, kind], peer_on(kind, o))
+
+    def by_count(kind, one, sem):
+        place, every, _, chunks = takes[kind]
+        for here in (0, 1):
+            @pl.when((place % every == 0) if here else (place % every != 0))
+            def _():
+                whole(one(chunks - here), sem)
+
+    def do_sum3():
         for kind in (0, 1):
-            whole(got2.at[kind], s_recv.at[1, kind])
-        skel[0, y, :FEAT] = total(0, mid[0], got2).astype(BF)
-        skel[0, z, FEAT:] = total(1, mid[1], got2).astype(BF)
+            by_count(kind, lambda n: skel.at[0, 0, pl.ds(0, 16 * n)], s_recv.at[2, kind])
         p, w = skel.at[0, y, pl.ds(0, FEAT)], skel.at[0, z, pl.ds(FEAT, COLS)]
         for o in range(1, SIDE):
-            remote(p, p, s_send.at[2, 0], s_recv.at[2, 0], at_leaf(o, 0))
-            remote(w, w, s_send.at[2, 1], s_recv.at[2, 1], at_leaf(0, o))
+            remote(p, p, s_send.at[4, 0], s_recv.at[3, 0], at_leaf(o, 0))
+            remote(w, w, s_send.at[4, 1], s_recv.at[3, 1], at_leaf(0, o))
 
     others = (skel.at[0, pl.ds(0, 7), pl.ds(0, FEAT)], skel.at[0, pl.ds(0, 7), pl.ds(FEAT, COLS)])
+
+    def hand_on(slot, part_of, k):
+        remote(skel.at[slot, part_of], skel.at[slot + 1, part_of], s_send.at[3, 0],
+               x_recv.at[slot + 1, k], at_grp(0, 1))
+
+    halves = (pl.ds(0, 4), pl.ds(4, 4))
 
     def do_own():
         for kind in (0, 1):
-            whole(others[kind], s_recv.at[2, kind])
-        for dx in (1, 3):
-            there = 2 * (4 - dx)
-            remote(skel.at[0], skel.at[there], s_send.at[3, 0], x_recv.at[there], at_grp(dx, 0))
-        remote(skel.at[0], skel.at[1], s_send.at[3, 0], x_recv.at[1], at_grp(0, 1))
-
-    def do_x(dx):
-        if dx != 2:
-            whole(skel.at[2 * dx], x_recv.at[2 * dx])
-            part_of = pl.ds(0 if dx == 1 else 4, 4)
-            remote(skel.at[2 * dx, part_of], skel.at[4, part_of], s_send.at[3, 1],
-                   x_recv.at[4 if dx == 1 else 8], at_grp(4 - dx, 0))
-        else:
-            whole(skel.at[4, pl.ds(0, 4)], x_recv.at[4])
-            whole(skel.at[4, pl.ds(4, 4)], x_recv.at[8])
-        remote(skel.at[2 * dx], skel.at[2 * dx + 1], s_send.at[3, 0], x_recv.at[2 * dx + 1], at_grp(0, 1))
+            whole(others[kind], s_recv.at[3, kind])
+        for first in (0, 1):
+            for dx in (1, 3):
+                there, k = 2 * (4 - dx), first if dx == 3 else 1 - first
+                remote(skel.at[0, halves[k]], skel.at[there, halves[k]], s_send.at[3, 0],
+                       x_recv.at[there, k], at_grp(dx, 0))
+        for k in (0, 1):
+            hand_on(0, halves[k], k)
+
+    def do_relay(dx):
+        k = 0 if dx == 1 else 1
+        whole(skel.at[2 * dx, halves[k]], x_recv.at[2 * dx, k])
+        remote(skel.at[2 * dx, halves[k]], skel.at[4, halves[k]], s_send.at[3, 1],
+               x_recv.at[4, k], at_grp(4 - dx, 0))
+        hand_on(2 * dx, halves[k], k)
+
+    def do_rest(dx):
+        k = 1 if dx == 1 else 0
+        whole(skel.at[2 * dx, halves[k]], x_recv.at[2 * dx, k])
+        hand_on(2 * dx, halves[k], k)
+
+    def do_last():
+        for k in (0, 1):
+            whole(skel.at[4, halves[k]], x_recv.at[4, k])
+            hand_on(4, halves[k], k)
 
     def block(xs, ws):
         rhs = jnp.concatenate([xs, aug_rows(half_norm(xs), 0)], axis=0)
@@ -304,15 +354,18 @@
 
     def do_far(rel):
         if rel % 2 == 1:
-            whole(skel.at[rel], x_recv.at[rel])
+            for k in (0, 1):
+                whole(skel.at[rel, halves[k]], x_recv.at[rel, k])
         both = jnp.concatenate([skel[rel, i] for i in range(SIDE)], axis=1)
         acc[...] += (block(both[:FEAT, :PTS], both[FEAT:, :PTS])
                      + block(both[:FEAT, PTS:], both[FEAT:, PTS:]))
 
     work = {"wait": do_wait, "send": do_send, "part": do_part, "sum1": do_sum1,
-            "sum2": do_sum2, "own": do_own, "targets": do_targets, "self": do_self}
-    for dx in (1, 2, 3):
-        work["x%d" % dx] = functools.partial(do_x, dx)
+            "sum2": do_sum2, "sum3": do_sum3, "own": do_own, "targets": do_targets, "self": do_self}
+    for dx in (1, 3):
+        work["relay%d" % dx] = functools.partial(do_relay, dx)
+        work["rest%d" % dx] = functools.partial(do_rest, dx)
+    work["last"] = do_last
     for rel in range(1, 8):
         work["far%d" % rel] = functools.partial(do_far, rel)
     for name, *args in schedule()[0]:
@@ -341,8 +394,14 @@
     whole(gat.at[pl.ds(0, 63)], g_send)
     for kind in (0, 1):
         whole(got1.at[kind], s_send.at[0, kind])
-        whole(got2.at[kind], s_send.at[1, kind])
-        whole(others[kind], s_send.at[2, kind])
+        by_count(kind, lambda n: (mid_p, mid_w)[kind].at[pl.ds(0, 16 * n)], s_send.at[1, kind])
+        place, every, _, _ = takes[kind]
+
+        @pl.when(place % every == 0)
+        def _():
+            whole(skel.at[0, 0:7, pl.ds(0, 16)], s_send.at[2, kind])
+
+        whole(others[kind], s_send.at[4, kind])
     whole(skel.at[pl.ds(0, 6)], s_send.at[3, 0])
     whole(skel.at[0], s_send.at[3, 1])
 
@@ -362,17 +421,19 @@
             pltpu.VMEM((1, SKEL), jnp.int32),
             pltpu.VMEM((2, SIDE, FEAT, PIECE), BF),
             pltpu.VMEM((2, SIDE - 1, FEAT, PIECE), BF),
-            pltpu.VMEM((2, FEAT, PIECE), BF),
-            pltpu.VMEM((2, SIDE - 1, FEAT, PIECE), BF),
+            pltpu.VMEM((FEAT, PIECE), BF),
+            pltpu.VMEM((COLS, PIECE), F32),
+            pltpu.VMEM((SIDE - 1, 16, PIECE), BF),
+            pltpu.VMEM((SIDE - 1, 16, PIECE), F32),
             pltpu.VMEM((8, SIDE, ROWS, PIECE), BF),
             pltpu.VMEM((PTS, FEAT + 16), BF),
             pltpu.VMEM((PTS, COLS), F32),
             pltpu.SemaphoreType.DMA((6,)),
             pltpu.SemaphoreType.DMA,
             pltpu.SemaphoreType.DMA((2, 64)),
+            pltpu.SemaphoreType.DMA((5, 2)),
             pltpu.SemaphoreType.DMA((4, 2)),
-            pltpu.SemaphoreType.DMA((3, 2)),
-            pltpu.SemaphoreType.DMA((9,)),
+            pltpu.SemaphoreType.DMA((8, 2)),
         ],
         cost_estimate=pl.CostEstimate(
             flops=flops, bytes_accessed=2 * PTS * SKEL, transcendentals=30 * PTS * PTS

time: 66.2 us -> 63.7 us (0.962)
  Pallas kernels: 64.5 us -> 62 us
    pallas_call x1, Pallas kernels: 64.5 us -> 62 us  [per_device(): pl.pallas_call(kernel, out_shape=jax.ShapeDtypeStruct((COLS, PTS), F32),...]
where the time goes in v3:
time: 63.7 us; the launch traced here: 63.5 us
  Pallas kernels  62 us (97%)
  local copies, waits for them, and re-layouts  1.47 us (2%)
    pallas_call x1, Pallas kernels, per_device(): pl.pallas_call(kernel, out_shape=jax.ShapeDtypeStruct((COLS, PTS), F32),...  62 us
    unnamed x1, local copies, waits for them, and re-layouts  1.47 us

profile of v3, /device:TPU:6, one launch (start us, length us, event | category | flops | bytes accessed | tf_op | source)
XLA Modules:
  0.0 63.5 jit_solution(15517130705645278967)
XLA Ops:
  0.0 62.0 %shard_map.64 = f32[32,512]{1,0:T(8,128)} custom-call(s32[16,64]{1,0:T(8,128)} %bitcast.7, s32[64]{0:T(128)} %count_hbm.1, s32[1,1024]{1,0:T(1,128)} %index_hbm.1, bf16[64,512]{1,0:T(8,128)(2,1)} %bitcast.5, bf16[32,512]{1,0:T(8,128)(2,1)} %bitcast.6, bf16[512,1024]{1,0:T(8,128)(2,1)} %interp_ref.1), custom_call_target="tpu_custom_call" | custom-call | flops 1862270976 | bytes 1048576 | tf_op jit(solution)/shard_map/pallas_call | solution.py:411
  62.0 1.5 %copy.8 = f32[512,32]{0,1:T(8,128)} copy(f32[512,32]{0,1:T(8,128)} %bitcast.4) | data formatting | bytes 131072

commit v4 on v3

--- a/solution.py
+++ b/solution.py
@@ -375,18 +375,15 @@
     own[5].wait()
     mine = count_ref[leaf]
 
-    @pl.loop(0, SLOTS // 5)
-    def _(i):
-        add = jnp.zeros((PTS, COLS), F32)
-        for j in range(5):
-            k = 1 + 5 * i + j
-            source = near_ref[k, leaf]
-            sy = (source // SIDE + SIDE - y) % SIDE
-            sz = (source % SIDE + SIDE - z) % SIDE
-            got = gat[sy * SIDE + sz]
-            used = jnp.where(k < mine, 1.0, 0.0).astype(F32)
-            add = add + block(got[:FEAT], (got[FEAT:].astype(F32) * used).astype(BF))
-        acc[...] += add
+    add = jnp.zeros((PTS, COLS), F32)
+    for k in range(1, SLOTS):
+        source = near_ref[k, leaf]
+        sy = (source // SIDE + SIDE - y) % SIDE
+        sz = (source % SIDE + SIDE - z) % SIDE
+        got = gat[sy * SIDE + sz]
+        used = jnp.where(k < mine, 1.0, 0.0).astype(F32)
+        add = add + block(got[:FEAT], (got[FEAT:].astype(F32) * used).astype(BF))
+    acc[...] += add
 
     pad = jnp.zeros((PTS, 128 - COLS), F32)
     out_ref[...] = jnp.concatenate([acc[...], pad], axis=1).T[:COLS]
@@ -408,6 +405,7 @@
 
 def per_device(points, weights, interp, near_leaf, near_count, skel_index):
     flops = 2 * 30 * PTS * PTS * (FEAT + 16 + COLS) + 2 * PTS * SKEL * ROWS
+    given = (near_leaf.T, near_count, skel_index, points.T, weights.T, interp)
     out = pl.pallas_call(
         kernel,
         out_shape=jax.ShapeDtypeStruct((COLS, PTS), F32),
@@ -439,9 +437,9 @@
             flops=flops, bytes_accessed=2 * PTS * SKEL, transcendentals=30 * PTS * PTS
         ),
         compiler_params=pltpu.CompilerParams(
-            collective_id=0, has_side_effects=True, vmem_limit_bytes=60 * 1024 * 1024
+            collective_id=0, has_side_effects=True, vmem_limit_bytes=40 * 1024 * 1024
         ),
-    )(near_leaf.T, near_count, skel_index, points.T, weights.T, interp)
+    )(*[pltpu.with_memory_space_constraint(a, pltpu.HBM) for a in given])
     return out.T
 
 

time: 63.7 us -> 61.8 us (0.970)
  Pallas kernels: 62 us -> 61.1 us
  local copies, waits for them, and re-layouts: 1.47 us -> 0.63 us
    pallas_call x1, Pallas kernels: 62 us -> 61.1 us  [per_device(): pl.pallas_call(kernel, out_shape=jax.ShapeDtypeStruct((COLS, PTS), F32),...]
    unnamed x1, local copies, waits for them, and re-layouts: 1.47 us -> 0.63 us
where the time goes in v4:
time: 61.8 us; the launch traced here: 61.7 us
  Pallas kernels  61.1 us (99%)
  local copies, waits for them, and re-layouts  0.63 us (1%)
    pallas_call x1, Pallas kernels, per_device(): pl.pallas_call(kernel, out_shape=jax.ShapeDtypeStruct((COLS, PTS), F32),...  61.1 us

profile of v4, /device:TPU:6, one launch (start us, length us, event | category | flops | bytes accessed | tf_op | source)
XLA Modules:
  0.0 61.7 jit_solution(6499059475064398261)
XLA Ops:
  0.0 61.1 %shard_map.64 = f32[32,512]{1,0:T(8,128)S(1)} custom-call(s32[16,64]{1,0:T(8,128)} %bitcast.7, s32[64]{0:T(128)} %count_hbm.1, s32[1,1024]{1,0:T(1,128)} %index_hbm.1, bf16[64,512]{1,0:T(8,128)(2,1)} %bitcast.5, bf16[32,512]{1,0:T(8,128)(2,1)} %bitcast.6, bf16[512,1024]{1,0:T(8,128)(2,1)} %interp_ref.1), custom_call_target="tpu_custom_call" | custom-call | flops 1862270976 | bytes 1048576 | tf_op jit(solution)/shard_map/pallas_call | solution.py:409
  61.1 0.6 %copy.8 = f32[512,32]{0,1:T(8,128)} copy(f32[512,32]{0,1:T(8,128)S(1)} %bitcast.4) | data formatting | bytes 131072

commit v5 on v4

--- a/solution.py
+++ b/solution.py
@@ -15,6 +15,7 @@
 ROWS = FEAT + COLS
 HALF = ROWS // 2
 PIECE = SKEL // SIDE
+FARTHEST = (4, 3, 5, 2, 6, 1, 7)
 
 FIRST = ((4, 3), (3, 4))
 
@@ -223,24 +224,28 @@
         here = slot_of(half, o1, o2)
         whole(gat.at[here, pl.ds(half * HALF, HALF)], g_recv.at[half, here])
 
+    def scatter(kind, place):
+        for o in FARTHEST:
+            remote(part.at[kind, (place + o) % SIDE], got1.at[kind, 7 - o], s_send.at[0, kind],
+                   s_recv.at[0, kind], peer_on(1 - kind, o))
+
     def do_part():
         for c in own[:4]:
             c.wait()
         index = index_v[...] - leaf * PTS
         pick = lax.broadcasted_iota(jnp.int32, (PTS, SKEL), 0) == index
         pts = jnp.dot(gat[0, :FEAT], pick.astype(BF), preferred_element_type=F32).astype(BF)
+        for k in range(SIDE):
+            part[0, k] = pts[:, k * PIECE:(k + 1) * PIECE]
+        scatter(0, y)
         wts = jnp.dot(gat[0, FEAT:], interp_v[...], preferred_element_type=F32)
         hi = wts.astype(BF)
         lo = (wts - hi.astype(F32)).astype(BF)
         for k in range(SIDE):
             cols = slice(k * PIECE, (k + 1) * PIECE)
-            part[0, k] = pts[:, cols]
             part[1, k, :COLS] = hi[:, cols]
             part[1, k, COLS:] = lo[:, cols]
-        for o in range(1, SIDE):
-            for kind, place in ((0, y), (1, z)):
-                remote(part.at[kind, (place + o) % SIDE], got1.at[kind, 7 - o], s_send.at[0, kind],
-                       s_recv.at[0, kind], peer_on(1 - kind, o))
+        scatter(1, z)
 
     takes = ((z, 2, y, FEAT // 16), (y, 4, z, COLS // 16))
 
@@ -281,7 +286,7 @@
                     v = v + got[k].astype(F32)
                 mine = pl.ds(pl.multiple_of(kind * FEAT + row, 16), 16)
                 skel[0, piece, mine] = v.astype(BF)
-                for o in range(1, SIDE):
+                for o in FARTHEST:
                     ref = skel.at[0, piece, mine]
                     remote(ref, ref, s_send.at[2, kind], s_recv.at[2, kind], peer_on(kind, o))
 
@@ -296,7 +301,7 @@
         for kind in (0, 1):
             by_count(kind, lambda n: skel.at[0, 0, pl.ds(0, 16 * n)], s_recv.at[2, kind])
         p, w = skel.at[0, y, pl.ds(0, FEAT)], skel.at[0, z, pl.ds(FEAT, COLS)]
-        for o in range(1, SIDE):
+        for o in FARTHEST:
             remote(p, p, s_send.at[4, 0], s_recv.at[3, 0], at_leaf(o, 0))
             remote(w, w, s_send.at[4, 1], s_recv.at[3, 1], at_leaf(0, o))
 

time: 61.8 us -> 61.8 us (level)
  no operation moved by 1% of the time
where the time goes in v5:
time: 61.8 us; the launch traced here: 61.7 us
  Pallas kernels  61.1 us (99%)
  local copies, waits for them, and re-layouts  0.63 us (1%)
    pallas_call x1, Pallas kernels, per_device(): pl.pallas_call(kernel, out_shape=jax.ShapeDtypeStruct((COLS, PTS), F32),...  61.1 us

profile of v5, /device:TPU:6, one launch (start us, length us, event | category | flops | bytes accessed | tf_op | source)
XLA Modules:
  0.0 61.7 jit_solution(9637073584231610915)
XLA Ops:
  0.0 61.1 %shard_map.64 = f32[32,512]{1,0:T(8,128)S(1)} custom-call(s32[16,64]{1,0:T(8,128)} %bitcast.7, s32[64]{0:T(128)} %count_hbm.1, s32[1,1024]{1,0:T(1,128)} %index_hbm.1, bf16[64,512]{1,0:T(8,128)(2,1)} %bitcast.5, bf16[32,512]{1,0:T(8,128)(2,1)} %bitcast.6, bf16[512,1024]{1,0:T(8,128)(2,1)} %interp_ref.1), custom_call_target="tpu_custom_call" | custom-call | flops 1862270976 | bytes 1048576 | tf_op jit(solution)/shard_map/pallas_call | solution.py:414
  61.1 0.6 %copy.8 = f32[512,32]{0,1:T(8,128)} copy(f32[512,32]{0,1:T(8,128)S(1)} %bitcast.4) | data formatting | bytes 131072

commit v6 on v5

--- a/solution.py
+++ b/solution.py
@@ -17,7 +17,7 @@
 PIECE = SKEL // SIDE
 FARTHEST = (4, 3, 5, 2, 6, 1, 7)
 
-FIRST = ((4, 3), (3, 4))
+FIRST = ((3, 4), (4, 3))
 
 
 def second(o):

time: 61.8 us -> 61.7 us (level)
  no operation moved by 1% of the time
where the time goes in v6:
time: 61.7 us; the launch traced here: 61.6 us
  Pallas kernels  61 us (99%)
  local copies, waits for them, and re-layouts  0.63 us (1%)
    pallas_call x1, Pallas kernels, per_device(): pl.pallas_call(kernel, out_shape=jax.ShapeDtypeStruct((COLS, PTS), F32),...  61 us

profile of v6, /device:TPU:6, one launch (start us, length us, event | category | flops | bytes accessed | tf_op | source)
XLA Modules:
  0.0 61.6 jit_solution(15793097808951999805)
XLA Ops:
  0.0 61.0 %shard_map.64 = f32[32,512]{1,0:T(8,128)S(1)} custom-call(s32[16,64]{1,0:T(8,128)} %bitcast.7, s32[64]{0:T(128)} %count_hbm.1, s32[1,1024]{1,0:T(1,128)} %index_hbm.1, bf16[64,512]{1,0:T(8,128)(2,1)} %bitcast.5, bf16[32,512]{1,0:T(8,128)(2,1)} %bitcast.6, bf16[512,1024]{1,0:T(8,128)(2,1)} %interp_ref.1), custom_call_target="tpu_custom_call" | custom-call | flops 1862270976 | bytes 1048576 | tf_op jit(solution)/shard_map/pallas_call | solution.py:414
  61.0 0.6 %copy.8 = f32[512,32]{0,1:T(8,128)} copy(f32[512,32]{0,1:T(8,128)S(1)} %bitcast.4) | data formatting | bytes 131072
